TPU v7x, 128 devices: a whole 4x4x4 slice. The times are simulated.
128 devices in a mesh: dp: 8 (over z, core), tensor: 16 (over y, x).
Axes of the slice: x: 4, y: 4, z: 4, core: 2. Of those that a mesh axis runs over, the one named last changes fastest.
Arguments:
- h_in: bfloat16 [1024, 8192], P('dp'), may hold values from -6 to 6
- dout: bfloat16 [1024, 8192], P('dp'), may hold values from -6 to 6
- w_gate: bfloat16 [28672, 512], P('tensor'), may hold values from -0.25 to 0.25
- w_up: bfloat16 [28672, 512], P('tensor'), may hold values from -0.25 to 0.25
- w_down: bfloat16 [28672, 512], P('tensor'), may hold values from -0.125 to 0.125
- in_layout: int32 [224, 4], P('tensor'), may hold values from 0 to 63, all different within a row
- out_layout: int32 [224, 4], P('tensor'), may hold values from 0 to 63, all different within a row
Outputs:
- out: bfloat16 [1024, 8192], P('dp', 'tensor')
- dh: bfloat16 [1024, 8192], P('dp', 'tensor')
- grad_gate: float32 [224, 65536], P('tensor', 'dp')
- grad_up: float32 [224, 65536], P('tensor', 'dp')
- grad_down: float32 [224, 65536], P('tensor', 'dp')
Inputs may be any that keep to these rules, and one draw needn't show every extreme that they name: `in_layout`: each block row names 4 different blocks; every block is named by some block row. `out_layout`: each block row names 4 different blocks; every block is named by some block row.
All inputs are finite; a program needn't handle non-finite values.
Results may differ from a plain program's by a relative error of at most 0.018.
Values may be sent and summed in bfloat16 or wider, within the bound.
No kernel may reach another device: no remote copies, remote signals or barrier semaphores. Data moves between devices by JAX's collectives and lax.ppermute only.
A program may use at most 128 MiB of HBM per device.

v0:
```python
import jax
import jax.numpy as jnp
from jax import lax
from jax.sharding import PartitionSpec as P

D = 8192
BLK = 128
KB = 4


def block_sum(values, layout_flat, tokens, nblocks):
    empty = jnp.zeros((tokens, nblocks, BLK), jnp.float32)
    return empty.at[:, layout_flat].add(values).reshape(tokens, nblocks * BLK)


def shards(h_in, dout, w_gate, w_up, w_down, in_layout, out_layout):
    tokens = h_in.shape[0]
    rows_grp = in_layout.shape[0]
    nblocks = D // BLK
    lin_flat = in_layout.reshape(-1)
    lout_flat = out_layout.reshape(-1)
    wg = w_gate.reshape(rows_grp, BLK, KB * BLK)
    wu = w_up.reshape(rows_grp, BLK, KB * BLK)
    wd = w_down.reshape(rows_grp, BLK, KB * BLK)
    hx = jnp.take(h_in.reshape(tokens, nblocks, BLK), lin_flat, axis=1).reshape(
        tokens, rows_grp, KB * BLK
    )
    gate = jnp.einsum("trm,rim->tri", hx, wg, preferred_element_type=jnp.float32)
    up = jnp.einsum("trm,rim->tri", hx, wu, preferred_element_type=jnp.float32)
    sig = jax.nn.sigmoid(gate)
    act = gate * sig
    hidden = (act * up).astype(jnp.bfloat16)
    contrib = jnp.einsum("tri,rim->trm", hidden, wd, preferred_element_type=jnp.float32)
    partial_out = block_sum(contrib.reshape(tokens, rows_grp * KB, BLK), lout_flat, tokens, nblocks)
    partial_out = partial_out.astype(jnp.bfloat16).astype(jnp.float32)
    out = lax.psum_scatter(
        partial_out.astype(jnp.bfloat16), "tensor", scatter_dimension=1, tiled=True
    )
    dob = jnp.take(dout.reshape(tokens, nblocks, BLK), lout_flat, axis=1).reshape(
        tokens, rows_grp, KB * BLK
    )
    dhid = jnp.einsum("trm,rim->tri", dob, wd, preferred_element_type=jnp.float32)
    g_down = jnp.einsum("tri,trm->rim", hidden, dob, preferred_element_type=jnp.float32).reshape(
        rows_grp, -1
    )
    dgate = (dhid * up * sig * (1.0 + gate * (1.0 - sig))).astype(jnp.bfloat16)
    dup = (dhid * act).astype(jnp.bfloat16)
    g_gate = jnp.einsum("tri,trm->rim", dgate, hx, preferred_element_type=jnp.float32).reshape(
        rows_grp, -1
    )
    g_up = jnp.einsum("tri,trm->rim", dup, hx, preferred_element_type=jnp.float32).reshape(
        rows_grp, -1
    )
    summed_gate, summed_up, summed_down = (
        lax.psum(g_gate.astype(jnp.bfloat16), "dp").astype(jnp.float32),
        lax.psum(g_up.astype(jnp.bfloat16), "dp").astype(jnp.float32),
        lax.psum(g_down.astype(jnp.bfloat16), "dp").astype(jnp.float32),
    )
    share = summed_gate.shape[1] // lax.axis_size("dp")
    offset = lax.axis_index("dp") * share
    gate_part = lax.dynamic_slice_in_dim(summed_gate, offset, share, 1)
    up_part = lax.dynamic_slice_in_dim(summed_up, offset, share, 1)
    down_part = lax.dynamic_slice_in_dim(summed_down, offset, share, 1)
    dhx = jnp.einsum("tri,rim->trm", dgate, wg, preferred_element_type=jnp.float32)
    dhx = dhx + jnp.einsum("tri,rim->trm", dup, wu, preferred_element_type=jnp.float32)
    partial_dh = block_sum(dhx.reshape(tokens, rows_grp * KB, BLK), lin_flat, tokens, nblocks)
    partial_dh = partial_dh.astype(jnp.bfloat16).astype(jnp.float32)
    dh = lax.psum_scatter(
        partial_dh.astype(jnp.bfloat16), "tensor", scatter_dimension=1, tiled=True
    )
    return (out, dh, gate_part, up_part, down_part)


def solution(mesh):
    placed = (
        P("dp", None),
        P("dp", None),
        P("tensor", None),
        P("tensor", None),
        P("tensor", None),
        P("tensor", None),
        P("tensor", None),
    )
    return jax.shard_map(
        shards,
        mesh=mesh,
        in_specs=placed,
        out_specs=(
            P("dp", "tensor"),
            P("dp", "tensor"),
            P("tensor", "dp"),
            P("tensor", "dp"),
            P("tensor", "dp"),
        ),
        check_vma=False,
    )
```

profile of v0, /device:TPU:0, one launch (start us, length us, event | category | flops | bytes accessed | tf_op | source)
XLA Modules:
  0.0 268.9 jit_solution(1614522637076494654)
XLA Ops:
  8.1 0.9 copy.43
  9.0 0.8 copy.42
  9.9 4.1 %copy.44 = bf16[128,8192]{0,1:T(8,128)(2,1)} copy(bf16[128,8192]{1,0:T(8,128)(2,1)} %param.9) | data formatting | bytes 4194304 | tf_op args[0]
  14.0 4.1 %copy.45 = bf16[128,64,128]{2,0,1:T(8,128)(2,1)} copy(bf16[128,64,128]{0,2,1:T(8,128)(2,1)} %bitcast.76) | data formatting | bytes 4194304 | tf_op jit(solution)/shard_map/reshape | solution.py:25
  18.1 3.6 %gather_fusion = bf16[56,128,128]{2,1,0:T(8,128)(2,1)} fusion(bf16[128,64,128]{2,0,1:T(8,128)(2,1)} %copy.45, s32[1024]{0:T(1024)S(1)} %pad_clamp_fusion.1), kind=kCustom, calls=%fused_computation.clone | custom fusion | bytes 3670240 | tf_op jit(solution)/shard_map/jit(_take)/gather | solution.py:25
  21.7 3.0 %select_bitcast_fusion.1 = bf16[128,56,128]{2,0,1:T(8,128)(2,1)} fusion(bf16[56,128,128]{2,1,0:T(8,128)(2,1)} %gather_fusion, pred[56]{0:T(512)(128)(4,1)S(1)} %get-tuple-element.25), kind=kLoop, calls=%fused_computation.7 | loop fusion | flops 917504 | bytes 3670072 | tf_op jit(solution)/shard_map/jit(_take)/select_n | solution.py:25
  24.7 3.9 %copy.46 = bf16[128,56,128]{0,2,1:T(8,128)(2,1)} copy(bf16[128,56,128]{2,0,1:T(8,128)(2,1)} %select_bitcast_fusion.1) | data formatting | bytes 3670016 | tf_op jit(solution)/shard_map/jit(_take)/select_n | solution.py:25
  28.6 3.9 %convolution_bitcast_fusion.2 = f32[128,14,128]{2,0,1:T(8,128)} fusion(bf16[128,14,512]{0,2,1:T(8,128)(2,1)} %bitcast.62, bf16[14,128,512]{2,1,0:T(8,128)(2,1)} %bitcast.78), kind=kOutput, calls=%fused_computation.12 | convolution fusion | flops 234881024 | bytes 4587520 | tf_op jit(solution)/shard_map/trm,rim->tri/dot_general | solution.py:29
  32.5 1.7 convolution_bitcast_fusion.3
  34.2 4.1 %copy.54 = bf16[128,8192]{0,1:T(8,128)(2,1)} copy(bf16[128,8192]{1,0:T(8,128)(2,1)} %param.10) | data formatting | bytes 4194304 | tf_op args[1]
  38.3 4.1 %copy.55 = bf16[128,64,128]{2,0,1:T(8,128)(2,1)} copy(bf16[128,64,128]{0,2,1:T(8,128)(2,1)} %bitcast.77) | data formatting | bytes 4194304 | tf_op jit(solution)/shard_map/reshape | solution.py:39
  42.4 3.6 %gather_fusion.1 = bf16[56,128,128]{2,1,0:T(8,128)(2,1)} fusion(bf16[128,64,128]{2,0,1:T(8,128)(2,1)} %copy.55, s32[1024]{0:T(1024)S(1)} %pad_clamp_fusion), kind=kCustom, calls=%fused_computation.1.clone | custom fusion | bytes 3670240 | tf_op jit(solution)/shard_map/jit(_take)/gather | solution.py:39
  46.0 3.0 %select_bitcast_fusion = bf16[128,56,128]{2,0,1:T(8,128)(2,1)} fusion(bf16[56,128,128]{2,1,0:T(8,128)(2,1)} %gather_fusion.1, pred[56]{0:T(512)(128)(4,1)S(1)} %get-tuple-element.24), kind=kLoop, calls=%fused_computation.6 | loop fusion | flops 917504 | bytes 3670072 | tf_op jit(solution)/shard_map/jit(_take)/select_n | solution.py:39
  49.0 3.9 %copy.56 = bf16[128,56,128]{0,2,1:T(8,128)(2,1)} copy(bf16[128,56,128]{2,0,1:T(8,128)(2,1)} %select_bitcast_fusion) | data formatting | bytes 3670016 | tf_op jit(solution)/shard_map/jit(_take)/select_n | solution.py:39
  52.9 3.1 %multiply_convert_fusion = (bf16[128,14,128]{2,0,1:T(8,128)(2,1)S(1)}, bf16[128,14,128]{2,0,1:T(8,128)(2,1)S(1)}, bf16[128,14,128]{2,0,1:T(8,128)(2,1)S(1)}) fusion(f32[128,14,128]{2,0,1:T(8,128)} %convolution_bitcast_fusion.3, f32[128,14,128]{2,0,1:T(8,128)} %convolution_bitcast_fusion.2, bf16[128,14,512]{0,2,1:T(8,128)(2,1)} %bitcast.82, ...), kind=kOutput, calls=%fused_computation.14 | convolution fusion | flops 238321664 | bytes 6881280 | tf_op jit(solution)/shard_map/trm,rim->tri/dot_general | solution.py:42
  55.9 0.7 convolution_convert_fusion.2
  56.6 0.2 pad.2
  56.9 2.6 copy.78
  59.4 0.7 convolution_convert_fusion.1
  60.1 0.2 pad.3
  60.4 2.5 copy.79
  62.9 0.7 convolution_convert_fusion
  63.6 0.2 pad.4
  63.8 2.5 copy.80
  66.3 0.2 reduce-scatter.5.cloned.1.call-start
  66.7 2.3 fusion.3
  69.0 2.5 add_bitcast_fusion
  71.5 5.1 %copy.58 = f32[128,14,512]{0,2,1:T(8,128)} copy(f32[128,14,512]{2,0,1:T(8,128)} %add_bitcast_fusion) | data formatting | bytes 7340032 | tf_op jit(solution)/shard_map/add | solution.py:65
  76.6 5.5 %copy.59 = f32[56,128,128]{2,1,0:T(8,128)} copy(f32[56,128,128]{1,2,0:T(8,128)} %bitcast.66) | data formatting | bytes 7340032 | tf_op jit(solution)/shard_map/reshape | solution.py:66
  82.0 2.5 broadcast.43.clone.1
  84.5 13.5 %scatter_fusion.1 = f32[128,64,128]{2,0,1:T(8,128)} fusion(f32[128,64,128]{2,0,1:T(8,128)} %broadcast.43.clone.1, s32[56]{0:T(128)S(1)} %get-tuple-element.27, f32[56,128,128]{2,1,0:T(8,128)} %copy.59), kind=kCustom, calls=%fused_computation.3 | custom fusion | flops 917504 | bytes 11010272 | tf_op jit(solution)/shard_map/scatter-add | solution.py:13
  98.0 4.0 %convert_element_type.57 = bf16[128,64,128]{2,0,1:T(8,128)(2,1)} convert(f32[128,64,128]{2,0,1:T(8,128)} %scatter_fusion.1) | non-fusion elementwise | flops 1048576 | bytes 6291456 | tf_op jit(solution)/shard_map/convert_element_type | solution.py:67
  102.0 4.1 %copy.60 = bf16[128,64,128]{0,2,1:T(8,128)(2,1)} copy(bf16[128,64,128]{2,0,1:T(8,128)(2,1)} %convert_element_type.57) | data formatting | bytes 4194304 | tf_op jit(solution)/shard_map/convert_element_type | solution.py:67
  106.2 2.5 convolution_bitcast_fusion
  108.6 5.1 %copy.49 = f32[128,14,512]{0,2,1:T(8,128)} copy(f32[128,14,512]{2,0,1:T(8,128)} %convolution_bitcast_fusion) | data formatting | bytes 7340032 | tf_op jit(solution)/shard_map/tri,rim->trm/transpose | solution.py:33
  113.7 5.2 %copy.50 = f32[56,128,128]{2,1,0:T(8,128)} copy(f32[56,128,128]{1,2,0:T(8,128)} %bitcast.67) | data formatting | bytes 7340032 | tf_op jit(solution)/shard_map/reshape | solution.py:34
  119.0 2.5 broadcast.43.clone
  121.4 13.6 %scatter_fusion = f32[128,64,128]{2,0,1:T(8,128)} fusion(f32[128,64,128]{2,0,1:T(8,128)} %broadcast.43.clone, s32[56]{0:T(128)S(1)} %get-tuple-element.26, f32[56,128,128]{2,1,0:T(8,128)} %copy.50), kind=kCustom, calls=%fused_computation.2 | custom fusion | flops 917504 | bytes 11010272 | tf_op jit(solution)/shard_map/scatter-add | solution.py:13
  135.0 4.0 %convert_element_type.53 = bf16[128,64,128]{2,0,1:T(8,128)(2,1)} convert(f32[128,64,128]{2,0,1:T(8,128)} %scatter_fusion) | non-fusion elementwise | flops 1048576 | bytes 6291456 | tf_op jit(solution)/shard_map/convert_element_type | solution.py:35
  139.0 4.2 %copy.51 = bf16[128,64,128]{0,2,1:T(8,128)(2,1)} copy(bf16[128,64,128]{2,0,1:T(8,128)(2,1)} %convert_element_type.53) | data formatting | bytes 4194304 | tf_op jit(solution)/shard_map/convert_element_type | solution.py:35
  143.2 10.7 %all-reduce.3.cloned.1.call-done = (bf16[14,65536]{1,0:T(8,128)(2,1)}, bf16[14,65536]{1,0:T(8,128)(2,1)}, bf16[14,65536]{1,0:T(8,128)(2,1)}) async-done(((bf16[14,65536]{1,0:T(8,128)(2,1)}, bf16[14,65536]{1,0:T(8,128)(2,1)}, bf16[14,65536]{1,0:T(8,128)(2,1)}), (bf16[14,65536]{1,0:T(8,128)(2,1)}, bf16[14,65536]{1,0:T(8,128)(2,1)}, bf16[14,65536]{1,0:T(8,128)(2,1)})) %all-reduce.3.cloned.1.call-update) | async-done | bytes 5505040 | tf_op jit(solution)/shard_map/psum | solution.py:55
  153.9 1.8 dynamic-slice_convert_fusion
  155.7 1.8 dynamic-slice_convert_fusion.1
  157.4 1.8 dynamic-slice_convert_fusion.2
  159.2 23.3 %reduce-scatter.5.cloned.1.call-done = bf16[128,512]{0,1:T(8,128)(2,1)} async-done(((bf16[128,8192]{0,1:T(8,128)(2,1)}), bf16[128,512]{0,1:T(8,128)(2,1)}) %reduce-scatter.5.cloned.1.call-update) | async-done | bytes 131088 | tf_op jit(solution)/shard_map/reduce_scatter | solution.py:68
  182.6 1.7 copy.68
  184.2 75.6 %reduce-scatter.3.cloned.1.call-done = bf16[128,512]{0,1:T(8,128)(2,1)} async-done(((bf16[128,8192]{0,1:T(8,128)(2,1)}), bf16[128,512]{0,1:T(8,128)(2,1)}) %reduce-scatter.3.cloned.1.call-update) | async-done | bytes 131088 | tf_op jit(solution)/shard_map/reduce_scatter | solution.py:36
  259.8 1.7 copy.67
  (26 shorter events, 0.5 us)
Async XLA Ops:
  8.0 44.9 %copy-start = (bf16[1792,512]{1,0:T(8,128)(2,1)S(1)}, bf16[1792,512]{1,0:T(8,128)(2,1)}, u32[]{:S(2)}) copy-start(bf16[1792,512]{1,0:T(8,128)(2,1)} %param.13) | copy-start | bytes 5505028
  8.0 145.9 %all-reduce.3.cloned.1.call-start = ((), (), s32[]{:S(2)}) async-start(), calls=%async_computation.4 | async-start | bytes 12582912 | tf_op jit(solution)/shard_map/psum | solution.py:55
  28.6 3.9 %copy-start.1 = (bf16[128,56,128]{0,2,1:T(8,128)(2,1)S(1)}, bf16[128,56,128]{0,2,1:T(8,128)(2,1)}, u32[]{:S(2)}) copy-start(bf16[128,56,128]{0,2,1:T(8,128)(2,1)} %copy.46) | copy-start | bytes 5505028
  28.6 3.9 %copy-start.4 = (bf16[1792,512]{1,0:T(8,128)(2,1)S(1)}, bf16[1792,512]{1,0:T(8,128)(2,1)}, u32[]{:S(2)}) copy-start(bf16[1792,512]{1,0:T(8,128)(2,1)} %param.11) | copy-start | bytes 5505028
  52.8 3.1 %copy-start.2 = (bf16[128,56,128]{0,2,1:T(8,128)(2,1)S(1)}, bf16[128,56,128]{0,2,1:T(8,128)(2,1)}, u32[]{:S(2)}) copy-start(bf16[128,56,128]{0,2,1:T(8,128)(2,1)} %copy.46) | copy-start | bytes 5505028
  60.4 2.5 copy-start.5
  66.3 116.3 %reduce-scatter.5.cloned.1.call-start = ((), (), s32[]{:S(2)}) async-start(), calls=%async_computation.3 | async-start | bytes 2228224 | tf_op jit(solution)/shard_map/reduce_scatter | solution.py:68
  66.7 2.3 copy-start.3
  106.1 153.7 %reduce-scatter.3.cloned.1.call-start = ((), (), s32[]{:S(2)}) async-start(), calls=%async_computation.2 | async-start | bytes 2228224 | tf_op jit(solution)/shard_map/reduce_scatter | solution.py:36
Sparse Core Ops, SparseCore 0:
  66.4 87.4 all-reduce.2
Sparse Core Ops, SparseCore 1:
  106.2 76.3 reduce-scatter.4
  186.0 73.7 reduce-scatter.2
where the time goes:
time: 270 us; the launch traced here: 269 us
  waiting for transfers between devices  110 us (41%)
  local copies, waits for them, and re-layouts  79 us (29%)
  other arithmetic  46.3 us (17%)
  matrix products  18 us (7%)
  between operations  15.6 us (6%)
    reduce_scatter x1, waiting for transfers between devices, shards(): lax.psum_scatter(partial_out.astype(jnp.bfloat16), 'tensor', scatter_dime...  75.6 us
    scatter-add x2, other arithmetic, block_sum(): return empty.at[:, layout_flat].add(values).reshape(tokens, nblocks * BLK)  27.1 us
    reduce_scatter x1, waiting for transfers between devices, shards(): lax.psum_scatter(partial_dh.astype(jnp.bfloat16), 'tensor', scatter_dimen...  23.3 us
    unnamed x24, local copies, waits for them, and re-layouts  21.4 us
    psum x1, waiting for transfers between devices, shards(): lax.psum(g_gate.astype(jnp.bfloat16), 'dp').astype(jnp.float32)  10.7 us
    reshape x1, local copies, waits for them, and re-layouts, shards(): dhx.reshape(tokens, rows_grp * KB, BLK)  5.46 us
  transfers between devices with their start and end apart: 3, of which 3 were waited for; matrix products, arithmetic and copies ran while one was open for 31% of the time, Pallas kernels for 0%

commit v1 on v0

--- a/solution.py
+++ b/solution.py
@@ -6,6 +6,12 @@
 D = 8192
 BLK = 128
 KB = 4
+
+
+def gather_and_add(value, axis):
+    parts = lax.all_gather(value, axis, axis=0, tiled=False)
+    total = parts.sum(axis=0)
+    return total
 
 
 def block_sum(values, layout_flat, tokens, nblocks):
@@ -52,7 +58,7 @@
         rows_grp, -1
     )
     summed_gate, summed_up, summed_down = (
-        lax.psum(g_gate.astype(jnp.bfloat16), "dp").astype(jnp.float32),
+        gather_and_add(g_gate.astype(jnp.bfloat16), "dp").astype(jnp.float32),
         lax.psum(g_up.astype(jnp.bfloat16), "dp").astype(jnp.float32),
         lax.psum(g_down.astype(jnp.bfloat16), "dp").astype(jnp.float32),
     )

time: 270 us -> 280 us (1.037)
  other arithmetic: 46.3 us -> 57.2 us
  waiting for transfers between devices: 110 us -> 105 us
    reduce_sum x0 -> x1, other arithmetic: none -> 11 us  [gather_and_add(): total = parts.sum(axis=0)]
    psum x1, waiting for transfers between devices: 10.7 us -> 0.02 us  [shards(): lax.psum(g_up.astype(jnp.bfloat16), 'dp').astype(jnp.float32)]
    reduce_scatter x1, waiting for transfers between devices: 23.3 us -> 29.2 us  [shards(): lax.psum_scatter(partial_dh.astype(jnp.bfloat16), 'tensor', scatter_dimen...]
    convert_element_type x0 -> x1, local copies, waits for them, and re-layouts: none -> 3.17 us  [shards(): g_gate.astype(jnp.bfloat16)]
    unnamed x24 -> x22, local copies, waits for them, and re-layouts: 21.4 us -> 18.7 us
  transfers between devices with their start and end apart: 3 -> 4, of which waited for: 3 -> 2; matrix products, arithmetic and copies ran while one was open for 31% -> 32% of each run, Pallas kernels for 0% -> 0%
where the time goes in v1:
time: 280 us; the launch traced here: 278 us
  waiting for transfers between devices  105 us (38%)
  local copies, waits for them, and re-layouts  79.5 us (28%)
  other arithmetic  57.2 us (20%)
  matrix products  20.5 us (7%)
  between operations  15.6 us (6%)
    reduce_scatter x1, waiting for transfers between devices, shards(): lax.psum_scatter(partial_out.astype(jnp.bfloat16), 'tensor', scatter_dime...  75.5 us
    reduce_scatter x1, waiting for transfers between devices, shards(): lax.psum_scatter(partial_dh.astype(jnp.bfloat16), 'tensor', scatter_dimen...  29.2 us
    scatter-add x2, other arithmetic, block_sum(): return empty.at[:, layout_flat].add(values).reshape(tokens, nblocks * BLK)  27 us
    unnamed x22, local copies, waits for them, and re-layouts  18.7 us
    reduce_sum x1, other arithmetic, gather_and_add(): total = parts.sum(axis=0)  11 us
  transfers between devices with their start and end apart: 4, of which 2 were waited for; matrix products, arithmetic and copies ran while one was open for 32% of the time, Pallas kernels for 0%

profile of v1, /device:TPU:0, one launch (start us, length us, event | category | flops | bytes accessed | tf_op | source)
XLA Modules:
  0.0 278.1 jit_solution(3761433038064757085)
XLA Ops:
  8.1 0.9 copy.70
  9.0 0.1 reshape.130
  9.0 0.8 copy.69
  9.9 4.1 %copy.71 = bf16[128,8192]{0,1:T(8,128)(2,1)} copy(bf16[128,8192]{1,0:T(8,128)(2,1)} %param.9) | data formatting | bytes 4194304 | tf_op args[0]
  14.0 4.1 %copy.72 = bf16[128,64,128]{2,0,1:T(8,128)(2,1)} copy(bf16[128,64,128]{0,2,1:T(8,128)(2,1)} %bitcast.71) | data formatting | bytes 4194304 | tf_op jit(solution)/shard_map/reshape | solution.py:31
  18.1 3.6 %gather_fusion = bf16[56,128,128]{2,1,0:T(8,128)(2,1)} fusion(bf16[128,64,128]{2,0,1:T(8,128)(2,1)} %copy.72, s32[1024]{0:T(1024)S(1)} %pad_clamp_fusion.1), kind=kCustom, calls=%fused_computation.clone | custom fusion | bytes 3670240 | tf_op jit(solution)/shard_map/jit(_take)/gather | solution.py:31
  21.7 3.0 %select_bitcast_fusion.1 = bf16[128,56,128]{2,0,1:T(8,128)(2,1)} fusion(bf16[56,128,128]{2,1,0:T(8,128)(2,1)} %gather_fusion, pred[56]{0:T(512)(128)(4,1)S(1)} %get-tuple-element.29), kind=kLoop, calls=%fused_computation.7 | loop fusion | flops 917504 | bytes 3670072 | tf_op jit(solution)/shard_map/jit(_take)/select_n | solution.py:31
  24.7 3.9 %copy.73 = bf16[128,56,128]{0,2,1:T(8,128)(2,1)} copy(bf16[128,56,128]{2,0,1:T(8,128)(2,1)} %select_bitcast_fusion.1) | data formatting | bytes 3670016 | tf_op jit(solution)/shard_map/jit(_take)/select_n | solution.py:31
  28.6 3.9 %convolution_bitcast_fusion.2 = f32[128,14,128]{2,0,1:T(8,128)} fusion(bf16[128,14,512]{0,2,1:T(8,128)(2,1)} %bitcast.59, bf16[14,128,512]{2,1,0:T(8,128)(2,1)} %bitcast.73), kind=kOutput, calls=%fused_computation.12 | convolution fusion | flops 234881024 | bytes 4587520 | tf_op jit(solution)/shard_map/trm,rim->tri/dot_general | solution.py:35
  32.4 1.6 convolution_bitcast_fusion.3
  34.1 4.1 %copy.81 = bf16[128,8192]{0,1:T(8,128)(2,1)} copy(bf16[128,8192]{1,0:T(8,128)(2,1)} %param.10) | data formatting | bytes 4194304 | tf_op args[1]
  38.2 4.1 %copy.82 = bf16[128,64,128]{2,0,1:T(8,128)(2,1)} copy(bf16[128,64,128]{0,2,1:T(8,128)(2,1)} %bitcast.72) | data formatting | bytes 4194304 | tf_op jit(solution)/shard_map/reshape | solution.py:45
  42.3 3.6 %gather_fusion.1 = bf16[56,128,128]{2,1,0:T(8,128)(2,1)} fusion(bf16[128,64,128]{2,0,1:T(8,128)(2,1)} %copy.82, s32[1024]{0:T(1024)S(1)} %pad_clamp_fusion), kind=kCustom, calls=%fused_computation.1.clone | custom fusion | bytes 3670240 | tf_op jit(solution)/shard_map/jit(_take)/gather | solution.py:45
  45.9 3.0 %select_bitcast_fusion = bf16[128,56,128]{2,0,1:T(8,128)(2,1)} fusion(bf16[56,128,128]{2,1,0:T(8,128)(2,1)} %gather_fusion.1, pred[56]{0:T(512)(128)(4,1)S(1)} %get-tuple-element.28), kind=kLoop, calls=%fused_computation.6 | loop fusion | flops 917504 | bytes 3670072 | tf_op jit(solution)/shard_map/jit(_take)/select_n | solution.py:45
  48.8 3.9 %copy.83 = bf16[128,56,128]{0,2,1:T(8,128)(2,1)} copy(bf16[128,56,128]{2,0,1:T(8,128)(2,1)} %select_bitcast_fusion) | data formatting | bytes 3670016 | tf_op jit(solution)/shard_map/jit(_take)/select_n | solution.py:45
  52.7 3.1 %multiply_convert_fusion = (bf16[128,14,128]{2,0,1:T(8,128)(2,1)S(1)}, bf16[128,14,128]{2,0,1:T(8,128)(2,1)S(1)}, bf16[128,14,128]{2,0,1:T(8,128)(2,1)S(1)}) fusion(f32[128,14,128]{2,0,1:T(8,128)} %convolution_bitcast_fusion.3, f32[128,14,128]{2,0,1:T(8,128)} %convolution_bitcast_fusion.2, bf16[128,14,512]{0,2,1:T(8,128)(2,1)} %bitcast.77, ...), kind=kOutput, calls=%fused_computation.14 | convolution fusion | flops 238321664 | bytes 6881280 | tf_op jit(solution)/shard_map/trm,rim->tri/dot_general | solution.py:48
  55.8 0.7 convolution_convert_fusion.1
  56.5 0.2 pad.2
  56.8 2.5 copy.105
  59.3 0.7 convolution_convert_fusion
  60.0 0.2 pad.3
  60.2 2.5 copy.106
  62.7 0.2 reduce-scatter.5.cloned.1.call-start
  63.2 2.3 fusion.3
  65.4 2.5 add_bitcast_fusion
  67.9 5.1 %copy.85 = f32[128,14,512]{0,2,1:T(8,128)} copy(f32[128,14,512]{2,0,1:T(8,128)} %add_bitcast_fusion) | data formatting | bytes 7340032 | tf_op jit(solution)/shard_map/add | solution.py:71
  73.0 5.4 %copy.86 = f32[56,128,128]{2,1,0:T(8,128)} copy(f32[56,128,128]{1,2,0:T(8,128)} %bitcast.63) | data formatting | bytes 7340032 | tf_op jit(solution)/shard_map/reshape | solution.py:72
  78.4 2.5 broadcast.43.clone.1
  80.8 13.4 %scatter_fusion.1 = f32[128,64,128]{2,0,1:T(8,128)} fusion(f32[128,64,128]{2,0,1:T(8,128)} %broadcast.43.clone.1, s32[56]{0:T(128)S(1)} %get-tuple-element.31, f32[56,128,128]{2,1,0:T(8,128)} %copy.86), kind=kCustom, calls=%fused_computation.3 | custom fusion | flops 917504 | bytes 11010272 | tf_op jit(solution)/shard_map/scatter-add | solution.py:19
  94.3 4.0 %convert_element_type.66 = bf16[128,64,128]{2,0,1:T(8,128)(2,1)} convert(f32[128,64,128]{2,0,1:T(8,128)} %scatter_fusion.1) | non-fusion elementwise | flops 1048576 | bytes 6291456 | tf_op jit(solution)/shard_map/convert_element_type | solution.py:73
  98.2 4.1 %copy.87 = bf16[128,64,128]{0,2,1:T(8,128)(2,1)} copy(bf16[128,64,128]{2,0,1:T(8,128)(2,1)} %convert_element_type.66) | data formatting | bytes 4194304 | tf_op jit(solution)/shard_map/convert_element_type | solution.py:73
  102.4 2.5 convolution_bitcast_fusion
  104.8 5.1 %copy.76 = f32[128,14,512]{0,2,1:T(8,128)} copy(f32[128,14,512]{2,0,1:T(8,128)} %convolution_bitcast_fusion) | data formatting | bytes 7340032 | tf_op jit(solution)/shard_map/tri,rim->trm/transpose | solution.py:39
  109.9 5.4 %copy.77 = f32[56,128,128]{2,1,0:T(8,128)} copy(f32[56,128,128]{1,2,0:T(8,128)} %bitcast.64) | data formatting | bytes 7340032 | tf_op jit(solution)/shard_map/reshape | solution.py:40
  115.3 2.5 broadcast.43.clone
  117.8 13.5 %scatter_fusion = f32[128,64,128]{2,0,1:T(8,128)} fusion(f32[128,64,128]{2,0,1:T(8,128)} %broadcast.43.clone, s32[56]{0:T(128)S(1)} %get-tuple-element.30, f32[56,128,128]{2,1,0:T(8,128)} %copy.77), kind=kCustom, calls=%fused_computation.2 | custom fusion | flops 917504 | bytes 11010272 | tf_op jit(solution)/shard_map/scatter-add | solution.py:19
  131.3 4.0 %convert_element_type.62 = bf16[128,64,128]{2,0,1:T(8,128)(2,1)} convert(f32[128,64,128]{2,0,1:T(8,128)} %scatter_fusion) | non-fusion elementwise | flops 1048576 | bytes 6291456 | tf_op jit(solution)/shard_map/convert_element_type | solution.py:41
  135.3 4.2 %copy.78 = bf16[128,64,128]{0,2,1:T(8,128)(2,1)} copy(bf16[128,64,128]{2,0,1:T(8,128)(2,1)} %convert_element_type.62) | data formatting | bytes 4194304 | tf_op jit(solution)/shard_map/convert_element_type | solution.py:41
  139.5 3.4 %convolution_convert_fusion.2 = bf16[14,128,512]{2,1,0:T(8,128)(2,1)} fusion(bf16[128,14,128]{2,0,1:T(8,128)(2,1)S(1)} %get-tuple-element.24, bf16[128,14,512]{0,2,1:T(8,128)(2,1)} %bitcast.60), kind=kOutput, calls=%fused_computation.10 | convolution fusion | flops 235798528 | bytes 4128768 | tf_op jit(solution)/shard_map/tri,trm->rim/dot_general | solution.py:54
  142.9 3.2 %convert_element_type.69 = bf16[1,14,65536]{2,1,0:T(8,128)(2,1)} reshape(bf16[14,128,512]{2,1,0:T(8,128)(2,1)} %convolution_convert_fusion.2) | data formatting | bytes 3670016 | tf_op jit(solution)/shard_map/convert_element_type | solution.py:61
  146.2 1.8 dynamic-slice_convert_fusion
  148.0 1.8 dynamic-slice_convert_fusion.1
  149.7 29.2 %reduce-scatter.5.cloned.1.call-done = bf16[128,512]{0,1:T(8,128)(2,1)} async-done(((bf16[128,8192]{0,1:T(8,128)(2,1)}), bf16[128,512]{0,1:T(8,128)(2,1)}) %reduce-scatter.5.cloned.1.call-update) | async-done | bytes 131088 | tf_op jit(solution)/shard_map/reduce_scatter | solution.py:74
  179.0 1.7 copy.95
  180.6 75.5 %reduce-scatter.3.cloned.1.call-done = bf16[128,512]{0,1:T(8,128)(2,1)} async-done(((bf16[128,8192]{0,1:T(8,128)(2,1)}), bf16[128,512]{0,1:T(8,128)(2,1)}) %reduce-scatter.3.cloned.1.call-update) | async-done | bytes 131088 | tf_op jit(solution)/shard_map/reduce_scatter | solution.py:42
  256.2 1.7 copy.94
  257.8 11.0 %reduce_sum.12 = bf16[14,65536]{1,0:T(8,128)(2,1)} reduce(bf16[8,14,65536]{2,1,0:T(8,128)(2,1)} %all-gather.2.cloned.1.call-done, bf16[]{:T(256)} %constant.11.clone.1), dimensions={0}, to_apply=%region_4.6 | reduce | flops 6422528 | bytes 16515074 | tf_op jit(solution)/shard_map/reduce_sum | solution.py:13
  268.9 1.8 dynamic-slice_convert_fusion.2
  (29 shorter events, 0.5 us)
Async XLA Ops:
  8.0 44.7 %copy-start = (bf16[1792,512]{1,0:T(8,128)(2,1)S(1)}, bf16[1792,512]{1,0:T(8,128)(2,1)}, u32[]{:S(2)}) copy-start(bf16[1792,512]{1,0:T(8,128)(2,1)} %param.13) | copy-start | bytes 5505028
  8.0 138.1 %all-reduce.3.cloned.1.call-start = ((), (), s32[]{:S(2)}) async-start(), calls=%async_computation.5 | async-start | bytes 8388608 | tf_op jit(solution)/shard_map/psum | solution.py:62
  28.6 3.9 %copy-start.1 = (bf16[128,56,128]{0,2,1:T(8,128)(2,1)S(1)}, bf16[128,56,128]{0,2,1:T(8,128)(2,1)}, u32[]{:S(2)}) copy-start(bf16[128,56,128]{0,2,1:T(8,128)(2,1)} %copy.73) | copy-start | bytes 5505028
  28.6 3.9 %copy-start.4 = (bf16[1792,512]{1,0:T(8,128)(2,1)S(1)}, bf16[1792,512]{1,0:T(8,128)(2,1)}, u32[]{:S(2)}) copy-start(bf16[1792,512]{1,0:T(8,128)(2,1)} %param.11) | copy-start | bytes 5505028
  52.7 3.1 %copy-start.2 = (bf16[128,56,128]{0,2,1:T(8,128)(2,1)S(1)}, bf16[128,56,128]{0,2,1:T(8,128)(2,1)}, u32[]{:S(2)}) copy-start(bf16[128,56,128]{0,2,1:T(8,128)(2,1)} %copy.73) | copy-start | bytes 5505028
  56.7 2.5 copy-start.5
  62.7 116.2 %reduce-scatter.5.cloned.1.call-start = ((), (), s32[]{:S(2)}) async-start(), calls=%async_computation.3 | async-start | bytes 2228224 | tf_op jit(solution)/shard_map/reduce_scatter | solution.py:74
  63.2 2.3 copy-start.3
  102.3 153.8 %reduce-scatter.3.cloned.1.call-start = ((), (), s32[]{:S(2)}) async-start(), calls=%async_computation.2 | async-start | bytes 2228224 | tf_op jit(solution)/shard_map/reduce_scatter | solution.py:42
  139.4 118.4 %all-gather.2.cloned.1.call-start = ((), (), s32[]{:S(2)}) async-start(), calls=%async_computation.4 | async-start | bytes 18874368 | tf_op jit(solution)/shard_map/all_gather | solution.py:12
Sparse Core Ops, SparseCore 0:
  62.9 75.9 all-reduce.2
  146.2 87.2 all-gather.1
Sparse Core Ops, SparseCore 1:
  102.4 76.5 reduce-scatter.4
  182.4 73.7 reduce-scatter.2
